TPU v7x, 32 devices: a whole 2x2x4 slice. The times are simulated.
32 devices in a mesh: dp: 8 (over z, y), tensor: 4 (over x, core).
Axes of the slice: x: 2, y: 2, z: 4, core: 2. Of those that a mesh axis runs over, the one named last changes fastest.
Arguments:
- tokens: bfloat16 [8192, 512], P('dp'), may hold values from -6 to 6
- memory: bfloat16 [8192, 512], P('dp'), may hold values from -6 to 6
- cotangent: bfloat16 [8192, 512], P('dp'), may hold values from -6 to 6
- lengths: int32 [16], P('dp'), may hold values from 1 to 512, 6144 in all
- breaks: int32 [16], P('dp'), may hold values from 1 to 501
- attn_in: float32 [6, 512, 512], P(None, 'dp', 'tensor'), may hold values from -0.25 to 0.25
- attn_out: float32 [2, 512, 512], P(None, 'dp', 'tensor'), may hold values from -3 to 3
- ffn_in: float32 [512, 2048], P('dp', 'tensor'), may hold values from -0.25 to 0.25
- ffn_out: float32 [512, 2048], P('dp', 'tensor'), may hold values from -0.125 to 0.125
- norms: float32 [6, 512], P(None, 'dp'), may hold values from -0.9 to 1.3, as said below
- attn_in_mom: float32 [6, 512, 512], P(None, 'dp', 'tensor'), may hold values from -256 to 256
- attn_out_mom: float32 [2, 512, 512], P(None, 'dp', 'tensor'), may hold values from -64 to 64
- ffn_in_mom: float32 [512, 2048], P('dp', 'tensor'), may hold values from -256 to 256
- ffn_out_mom: float32 [512, 2048], P('dp', 'tensor'), may hold values from -256 to 256
- norms_mom: float32 [6, 512], P(None, 'dp'), may hold values from -256 to 256
- attn_in_avg: float32 [6, 512, 512], P(None, 'dp', 'tensor'), may hold values from -0.25 to 0.25
- attn_out_avg: float32 [2, 512, 512], P(None, 'dp', 'tensor'), may hold values from -3 to 3
- ffn_in_avg: float32 [512, 2048], P('dp', 'tensor'), may hold values from -0.25 to 0.25
- ffn_out_avg: float32 [512, 2048], P('dp', 'tensor'), may hold values from -0.125 to 0.125
- norms_avg: float32 [6, 512], P(None, 'dp'), may hold values from 0.5 to 1.5
Outputs:
- block_out: bfloat16 [8192, 512], P('dp')
- tokens_grad: float32 [8192, 512], P('dp')
- attn_in_grad: float32 [6, 512, 512], P(None, 'dp', 'tensor')
- attn_in_mom_new: float32 [6, 512, 512], P(None, 'dp', 'tensor')
- attn_in_new: float32 [6, 512, 512], P(None, 'dp', 'tensor')
- attn_in_avg_new: float32 [6, 512, 512], P(None, 'dp', 'tensor')
- attn_out_grad: float32 [2, 512, 512], P(None, 'dp', 'tensor')
- attn_out_mom_new: float32 [2, 512, 512], P(None, 'dp', 'tensor')
- attn_out_new: float32 [2, 512, 512], P(None, 'dp', 'tensor')
- attn_out_avg_new: float32 [2, 512, 512], P(None, 'dp', 'tensor')
- ffn_in_grad: float32 [512, 2048], P('dp', 'tensor')
- ffn_in_mom_new: float32 [512, 2048], P('dp', 'tensor')
- ffn_in_new: float32 [512, 2048], P('dp', 'tensor')
- ffn_in_avg_new: float32 [512, 2048], P('dp', 'tensor')
- ffn_out_grad: float32 [512, 2048], P('dp', 'tensor')
- ffn_out_mom_new: float32 [512, 2048], P('dp', 'tensor')
- ffn_out_new: float32 [512, 2048], P('dp', 'tensor')
- ffn_out_avg_new: float32 [512, 2048], P('dp', 'tensor')
- norms_grad: float32 [6, 512], P(None, 'dp')
- norms_mom_new: float32 [6, 512], P(None, 'dp')
- norms_new: float32 [6, 512], P(None, 'dp')
- norms_avg_new: float32 [6, 512], P(None, 'dp')
Inputs may be any that keep to these rules, and one draw needn't show every extreme that they name: Positions at and beyond a protein's length are padding; the largest length is 512 in every draw, and the lengths sum to 6144. The linker slots breaks to breaks + 9 are padding between the first and the second chain; where they lie at or beyond the length the complex holds one chain. `norms`: rows 0, 2, 4 are gains, rows 1, 3, 5 biases.
All inputs are finite; a program needn't handle non-finite values. No bound on the sum of `lengths` on one device may be relied on, other than what follows from the above.
Results may differ from a plain program's by a relative error of at most 0.02.
The roundings to bfloat16 on the way count: a program that leaves them out, or rounds other values in their place, can miss the bound.
Values may be sent and summed in bfloat16 or wider, within the bound.
A program may use at most 128 MiB of HBM per device.

v0:
```python
from functools import partial
import jax
import jax.numpy as jnp
from jax import lax
from jax.sharding import PartitionSpec as P

HD = 64
SEQ = 512
LINKER = 10
EPSILON = 1e-05
NEG_FILL = -1000000000.0
MOMENTUM = 0.9
AVG_DECAY = 0.6
BASE_RATES = (0.05, 1.0, 0.05, 0.05, 0.3)


def layer_norm(values, gain_row, bias_row):
    center = values - jnp.mean(values, -1, keepdims=True)
    spread = jnp.mean(center * center, -1, keepdims=True)
    inv_std = lax.rsqrt(spread + EPSILON)
    x_hat = center * inv_std
    return (x_hat * gain_row + bias_row, x_hat, inv_std)


def norm_back(grad_h, x_hat, inv_std, gain_row):
    grad_gain = jnp.sum(grad_h * x_hat, 0)
    grad_bias = jnp.sum(grad_h, 0)
    grad_hat = grad_h * gain_row
    grad_in = inv_std * (
        grad_hat
        - jnp.mean(grad_hat, -1, keepdims=True)
        - x_hat * jnp.mean(grad_hat * x_hat, -1, keepdims=True)
    )
    return (grad_in, grad_gain, grad_bias)


def matmul_in(left_op, right_op):
    return jnp.dot(left_op, right_op, preferred_element_type=jnp.float32)


def matmul_tr(left_op, right_op):
    return lax.dot_general(
        left_op, right_op, (((1,), (1,)), ((), ())), preferred_element_type=jnp.float32
    )


def weight_grad(left_op, right_op):
    return lax.dot_general(
        left_op, right_op, (((0,), (0,)), ((), ())), preferred_element_type=jnp.float32
    )


def score_block(query, keys_b, mask_ok):
    seq_len = query.shape[0]
    query_h = query.reshape(seq_len, -1, HD)
    keys_h = keys_b.reshape(keys_b.shape[0], -1, HD)
    scores = jnp.einsum(
        "qhe,khe->hqk", query_h, keys_h, preferred_element_type=jnp.float32
    ) * HD ** (-0.5)
    return jnp.where(mask_ok[None], scores, NEG_FILL)


def attend_fwd(query, keys_b, values_b, mask_ok):
    seq_len = query.shape[0]
    scores = score_block(query, keys_b, mask_ok)
    top_score = jnp.max(scores, -1, keepdims=True)
    log_total = top_score + jnp.log(jnp.sum(jnp.exp(scores - top_score), -1, keepdims=True))
    prob_low = jnp.exp(scores - log_total).astype(jnp.bfloat16)
    values_h = values_b.reshape(values_b.shape[0], -1, HD)
    mixed = jnp.einsum("hqk,khe->qhe", prob_low, values_h, preferred_element_type=jnp.float32)
    return (mixed.reshape(seq_len, -1).astype(jnp.bfloat16), log_total)


def attend_back(grad_low, query, keys_b, values_b, log_total, mask_ok):
    seq_len = query.shape[0]
    scale_val = HD ** (-0.5)
    query_h = query.reshape(seq_len, -1, HD)
    keys_h = keys_b.reshape(keys_b.shape[0], -1, HD)
    values_h = values_b.reshape(values_b.shape[0], -1, HD)
    grad_h = grad_low.reshape(seq_len, -1, HD)
    attn_prob = jnp.exp(score_block(query, keys_b, mask_ok) - log_total)
    prob_low = attn_prob.astype(jnp.bfloat16)
    grad_prob = jnp.einsum("qhe,khe->hqk", grad_h, values_h, preferred_element_type=jnp.float32)
    inner_sum = jnp.sum(attn_prob * grad_prob, -1, keepdims=True)
    grad_score = (attn_prob * (grad_prob - inner_sum)).astype(jnp.bfloat16)
    grad_query = (
        jnp.einsum("hqk,khe->qhe", grad_score, keys_h, preferred_element_type=jnp.float32)
        * scale_val
    )
    grad_keys = (
        jnp.einsum("hqk,qhe->khe", grad_score, query_h, preferred_element_type=jnp.float32)
        * scale_val
    )
    grad_values = jnp.einsum("hqk,qhe->khe", prob_low, grad_h, preferred_element_type=jnp.float32)
    return (
        grad_query.reshape(seq_len, -1).astype(jnp.bfloat16),
        grad_keys.reshape(keys_b.shape[0], -1).astype(jnp.bfloat16),
        grad_values.reshape(values_b.shape[0], -1).astype(jnp.bfloat16),
    )


def update(weight, grad_sum, moment, average, rate):
    moment_new = MOMENTUM * moment + grad_sum
    weight_new = weight - rate * (grad_sum + MOMENTUM * moment_new)
    average_new = AVG_DECAY * average + (1.0 - AVG_DECAY) * weight_new
    return (grad_sum, moment_new, weight_new, average_new)


def per_device(
    tokens,
    memory,
    cotangent,
    lengths,
    breaks,
    attn_in,
    attn_out,
    ffn_in,
    ffn_out,
    norms,
    attn_in_mom,
    attn_out_mom,
    ffn_in_mom,
    ffn_out_mom,
    norms_mom,
    attn_in_avg,
    attn_out_avg,
    ffn_in_avg,
    ffn_out_avg,
    norms_avg,
):
    low_type = jnp.bfloat16
    in_rows, out_rows, norm_rows = (
        lax.all_gather(attn_in.astype(low_type), "dp", axis=1, tiled=True),
        lax.all_gather(attn_out.astype(low_type), "dp", axis=1, tiled=True),
        lax.all_gather(norms.astype(low_type), "dp", axis=1, tiled=True),
    )
    up_rows, down_rows = (
        lax.all_gather(ffn_in.astype(low_type), "dp", axis=0, tiled=True),
        lax.all_gather(ffn_out.astype(low_type), "dp", axis=0, tiled=True),
    )
    gain_all = norm_rows.astype(jnp.float32)
    gelu_fn = partial(jax.nn.gelu, approximate=False)

    def add_branch(resid, part_out):
        return resid + lax.psum(part_out, "tensor")

    def sum_grad(part_grad):
        return lax.psum(part_grad, "tensor")

    def protein_step(totals, item):
        tok_b, mem_b, cot_b, length_n, break_n = item
        tokens_f = tok_b.astype(jnp.float32)
        positions = jnp.arange(SEQ)
        linker = (positions >= break_n) & (positions < break_n + LINKER)
        live = (positions < length_n) & jnp.logical_not(linker)
        key_live = live[None, :]
        self_ok = (positions[None, :] <= positions[:, None]) & key_live
        cross_ok = jnp.broadcast_to(key_live, (SEQ, SEQ))
        h_one, hat_one, inv_one = layer_norm(tokens_f, gain_all[0], gain_all[1])
        h_one_b = h_one.astype(low_type)
        q_self = matmul_in(h_one_b, in_rows[0]).astype(low_type)
        k_self = matmul_in(h_one_b, in_rows[1]).astype(low_type)
        v_self = matmul_in(h_one_b, in_rows[2]).astype(low_type)
        a_self, lse_self = attend_fwd(q_self, k_self, v_self, self_ok)
        x_one = add_branch(tokens_f, matmul_tr(a_self, out_rows[0]))
        h_two, hat_two, inv_two = layer_norm(x_one, gain_all[2], gain_all[3])
        h_two_b = h_two.astype(low_type)
        q_cross = matmul_in(h_two_b, in_rows[3]).astype(low_type)
        k_cross = matmul_in(mem_b, in_rows[4]).astype(low_type)
        v_cross = matmul_in(mem_b, in_rows[5]).astype(low_type)
        a_cross, lse_cross = attend_fwd(q_cross, k_cross, v_cross, cross_ok)
        x_two = add_branch(x_one, matmul_tr(a_cross, out_rows[1]))
        h_three, hat_three, inv_three = layer_norm(x_two, gain_all[4], gain_all[5])
        h_three_b = h_three.astype(low_type)
        hidden = matmul_in(h_three_b, up_rows)
        act_low = gelu_fn(hidden).astype(low_type)
        out_part = add_branch(x_two, matmul_tr(act_low, down_rows))
        block_out = out_part.astype(low_type)
        row_live = live.astype(jnp.float32)[:, None]
        grad_out = cot_b.astype(jnp.float32) * row_live
        grad_z = grad_out.astype(low_type)
        grad_down = weight_grad(grad_z, act_low)
        grad_act = matmul_in(grad_z, down_rows)
        gelu_out, gelu_pull = jax.vjp(gelu_fn, hidden)
        grad_hidden = gelu_pull(grad_act)[0].astype(low_type)
        grad_up = weight_grad(h_three_b, grad_hidden)
        dh_three = sum_grad(matmul_tr(grad_hidden, up_rows))
        dx_norm3, gain_g3, bias_g3 = norm_back(dh_three, hat_three, inv_three, gain_all[4])
        dx_two = grad_out + dx_norm3
        dy_cross = dx_two.astype(low_type)
        grad_o_cross = weight_grad(dy_cross, a_cross)
        do_cross = matmul_in(dy_cross, out_rows[1]).astype(low_type)
        dq_cross, dk_cross, dv_cross = attend_back(
            do_cross, q_cross, k_cross, v_cross, lse_cross, cross_ok
        )
        grad_q_cross = weight_grad(h_two_b, dq_cross)
        grad_k_cross = weight_grad(mem_b, dk_cross)
        grad_v_cross = weight_grad(mem_b, dv_cross)
        dh_two = sum_grad(matmul_tr(dq_cross, in_rows[3]))
        dx_norm2, gain_g2, bias_g2 = norm_back(dh_two, hat_two, inv_two, gain_all[2])
        dx_one = dx_two + dx_norm2
        dy_self = dx_one.astype(low_type)
        grad_o_self = weight_grad(dy_self, a_self)
        do_self = matmul_in(dy_self, out_rows[0]).astype(low_type)
        dq_self, dk_self, dv_self = attend_back(do_self, q_self, k_self, v_self, lse_self, self_ok)
        grad_q_self = weight_grad(h_one_b, dq_self)
        grad_k_self = weight_grad(h_one_b, dk_self)
        grad_v_self = weight_grad(h_one_b, dv_self)
        dh_one = sum_grad(
            matmul_tr(dq_self, in_rows[0])
            + matmul_tr(dk_self, in_rows[1])
            + matmul_tr(dv_self, in_rows[2])
        )
        dx_norm1, gain_g1, bias_g1 = norm_back(dh_one, hat_one, inv_one, gain_all[0])
        tokens_grad = dx_one + dx_norm1
        grad_in_all = jnp.stack(
            [grad_q_self, grad_k_self, grad_v_self, grad_q_cross, grad_k_cross, grad_v_cross]
        )
        grad_out_all = jnp.stack([grad_o_self, grad_o_cross])
        grad_norm_all = jnp.stack([gain_g1, bias_g1, gain_g2, bias_g2, gain_g3, bias_g3])
        found = (grad_in_all, grad_out_all, grad_norm_all, grad_up, grad_down)
        return (jax.tree.map(jnp.add, totals, found), (block_out, tokens_grad))

    width = tokens.shape[1]
    count = tokens.shape[0] // SEQ
    items = (
        tokens.reshape(count, SEQ, width),
        memory.reshape(count, SEQ, width),
        cotangent.reshape(count, SEQ, width),
        lengths,
        breaks,
    )
    zeros_init = (
        jnp.zeros(in_rows.shape, jnp.float32),
        jnp.zeros(out_rows.shape, jnp.float32),
        jnp.zeros(norm_rows.shape, jnp.float32),
        jnp.zeros(up_rows.shape, jnp.float32),
        jnp.zeros(down_rows.shape, jnp.float32),
    )
    totals, (outs_all, grads_all) = lax.scan(protein_step, zeros_init, items)
    grad_in_all, grad_out_all, grad_norm_all, grad_up, grad_down = totals
    full_in, full_out, full_norm, full_up, full_down = lax.psum(
        (grad_in_all, grad_out_all, grad_norm_all, grad_up, grad_down), "dp"
    )
    owner = lax.axis_index("dp")
    own_rows = attn_in.shape[1]
    ffn_own = ffn_in.shape[0]
    shard_in = lax.dynamic_slice_in_dim(full_in, owner * own_rows, own_rows, 1)
    shard_out = lax.dynamic_slice_in_dim(full_out, owner * own_rows, own_rows, 1)
    shard_norm = lax.dynamic_slice_in_dim(full_norm, owner * norms.shape[1], norms.shape[1], 1)
    shard_up = lax.dynamic_slice_in_dim(full_up, owner * ffn_own, ffn_own, 0)
    shard_down = lax.dynamic_slice_in_dim(full_down, owner * ffn_own, ffn_own, 0)
    rate_scale = float(lax.axis_size("dp") * SEQ * count) ** (-0.5)
    in_g, in_m, in_w, in_a = update(
        attn_in, shard_in, attn_in_mom, attn_in_avg, BASE_RATES[0] * rate_scale
    )
    out_g, out_m, out_w, out_a = update(
        attn_out, shard_out, attn_out_mom, attn_out_avg, BASE_RATES[1] * rate_scale
    )
    up_g, up_m, up_w, up_a = update(
        ffn_in, shard_up, ffn_in_mom, ffn_in_avg, BASE_RATES[2] * rate_scale
    )
    down_g, down_m, down_w, down_a = update(
        ffn_out, shard_down, ffn_out_mom, ffn_out_avg, BASE_RATES[3] * rate_scale
    )
    norm_g, norm_m, norm_w, norm_a = update(
        norms, shard_norm, norms_mom, norms_avg, BASE_RATES[4] * rate_scale
    )
    return (
        outs_all.reshape(count * SEQ, width),
        grads_all.reshape(count * SEQ, width),
        in_g,
        in_m,
        in_w,
        in_a,
        out_g,
        out_m,
        out_w,
        out_a,
        up_g,
        up_m,
        up_w,
        up_a,
        down_g,
        down_m,
        down_w,
        down_a,
        norm_g,
        norm_m,
        norm_w,
        norm_a,
    )


def solution(mesh):
    return jax.shard_map(
        per_device,
        mesh=mesh,
        in_specs=(
            P("dp", None),
            P("dp", None),
            P("dp", None),
            P("dp"),
            P("dp"),
            P(None, "dp", "tensor"),
            P(None, "dp", "tensor"),
            P("dp", "tensor"),
            P("dp", "tensor"),
            P(None, "dp"),
            P(None, "dp", "tensor"),
            P(None, "dp", "tensor"),
            P("dp", "tensor"),
            P("dp", "tensor"),
            P(None, "dp"),
            P(None, "dp", "tensor"),
            P(None, "dp", "tensor"),
            P("dp", "tensor"),
            P("dp", "tensor"),
            P(None, "dp"),
        ),
        out_specs=(
            P("dp", None),
            P("dp", None),
            P(None, "dp", "tensor"),
            P(None, "dp", "tensor"),
            P(None, "dp", "tensor"),
            P(None, "dp", "tensor"),
            P(None, "dp", "tensor"),
            P(None, "dp", "tensor"),
            P(None, "dp", "tensor"),
            P(None, "dp", "tensor"),
            P("dp", "tensor"),
            P("dp", "tensor"),
            P("dp", "tensor"),
            P("dp", "tensor"),
            P("dp", "tensor"),
            P("dp", "tensor"),
            P("dp", "tensor"),
            P("dp", "tensor"),
            P(None, "dp"),
            P(None, "dp"),
            P(None, "dp"),
            P(None, "dp"),
        ),
        check_vma=False,
    )
```

profile of v0, /device:TPU:0, one launch (start us, length us, event | category | flops | bytes accessed | tf_op | source)
XLA Modules:
  0.0 873.6 jit_solution(5237097628865005914)
XLA Ops:
  8.9 27.8 %all-gather = bf16[8,64,6]{1,2,0:T(8,128)(2,1)S(1)} all-gather(bf16[1,64,6]{1,2,0:T(8,128)(2,1)S(1)} %convert_bitcast_fusion.1), channel_id=1, replica_groups=mesh['dp'=8,'tensor'=4] {'dp'}, dimensions={0}, use_global_device_ids=true | all-gather | bytes 6912 | tf_op jit(solution)/shard_map/all_gather | solution.py:135
  41.0 30.9 %all_gather.17 = bf16[2,512,128]{2,1,0:T(8,128)(2,1)S(1)} all-gather(bf16[2,64,128]{2,1,0:T(8,128)(2,1)S(1)} %convert_element_type.200), channel_id=1, replica_groups=mesh['dp'=8,'tensor'=4] {'dp'}, dimensions={1}, use_global_device_ids=true | all-gather | bytes 294912 | tf_op jit(solution)/shard_map/all_gather | solution.py:134
  71.8 33.4 %all_gather.19 = bf16[512,512]{1,0:T(8,128)(2,1)} all-gather(bf16[64,512]{1,0:T(8,128)(2,1)S(1)} %convert_element_type.202), channel_id=1, replica_groups=mesh['dp'=8,'tensor'=4] {'dp'}, dimensions={0}, use_global_device_ids=true | all-gather | bytes 589824 | tf_op jit(solution)/shard_map/all_gather | solution.py:139
  105.2 33.6 %all_gather.18 = bf16[512,512]{1,0:T(8,128)(2,1)} all-gather(bf16[64,512]{1,0:T(8,128)(2,1)S(1)} %convert_element_type.201), channel_id=1, replica_groups=mesh['dp'=8,'tensor'=4] {'dp'}, dimensions={0}, use_global_device_ids=true | all-gather | bytes 589824 | tf_op jit(solution)/shard_map/all_gather | solution.py:138
  138.7 33.6 %all_gather.16 = bf16[6,512,128]{2,1,0:T(8,128)(2,1)} all-gather(bf16[6,64,128]{2,1,0:T(8,128)(2,1)S(1)} %convert_element_type.199), channel_id=1, replica_groups=mesh['dp'=8,'tensor'=4] {'dp'}, dimensions={1}, use_global_device_ids=true | all-gather | bytes 884736 | tf_op jit(solution)/shard_map/all_gather | solution.py:133
  172.3 526.3 %while.23 = (s32[]{:T(128)}, f32[6,512,128]{2,1,0:T(8,128)}, f32[2,512,128]{2,1,0:T(8,128)}, f32[6,512]{1,0:T(8,128)}, f32[512,512]{1,0:T(8,128)}, /*index=5*/f3...) while((s32[]{:T(128)}, f32[6,512,128]{2,1,0:T(8,128)}, ...), condition=%wide.region_31.32_spmd.clone, body=%wide.region_0.31_spmd.clone.sunk | while | flops 3963490304 | bytes 262780928 | solution.py:240
  187.5 2.0 convolution_convert_fusion.30
  191.0 32.4 %all-reduce.13.cloned.1.call-done = f32[512,512]{1,0:T(8,128)} async-done(((f32[512,512]{1,0:T(8,128)}), f32[512,512]{1,0:T(8,128)}) %all-reduce.13.cloned.1.call-update) | async-done | bytes 1048592 | tf_op jit(solution)/shard_map/while/body/eval_jaxpr/psum | solution.py:145
  230.2 36.6 %all-reduce.15.cloned.1.call-done = f32[512,512]{1,0:T(8,128)} async-done(((f32[512,512]{1,0:T(8,128)}), f32[512,512]{1,0:T(8,128)}) %all-reduce.15.cloned.1.call-update) | async-done | bytes 1048592 | tf_op jit(solution)/shard_map/while/body/eval_jaxpr/psum | solution.py:145
  269.0 3.6 multiply_convert_fusion.6
  275.8 2.8 convolution_add_fusion.11
  281.9 30.5 %all-reduce.17.cloned.1.call-done = f32[512,512]{1,0:T(8,128)} async-done(((f32[512,512]{1,0:T(8,128)}), f32[512,512]{1,0:T(8,128)}) %all-reduce.17.cloned.1.call-update) | async-done | bytes 1048592 | tf_op jit(solution)/shard_map/while/body/eval_jaxpr/psum | solution.py:148
  312.4 2.5 multiply_reduce_fusion.19
  319.9 2.2 fusion.366
  322.2 2.4 fusion.373
  324.6 2.0 convolution_convert_fusion.35
  326.6 32.2 %all-reduce.19.cloned.1.call-done = f32[512,512]{1,0:T(8,128)} async-done(((f32[512,512]{1,0:T(8,128)}), f32[512,512]{1,0:T(8,128)}) %all-reduce.19.cloned.1.call-update) | async-done | bytes 1048592 | tf_op jit(solution)/shard_map/while/body/eval_jaxpr/psum | solution.py:148
  358.8 2.7 multiply_reduce_fusion.21
  372.2 2.2 convolution_add_fusion.9
  374.4 2.0 fusion.371
  378.3 2.1 fusion.374
  380.4 2.1 fusion.375
  382.7 3.0 select_add_fusion.4
  385.8 43.8 %all-reduce.21.cloned.1.call-done = (f32[512,512]{1,0:T(8,128)}, f32[512,512]{1,0:T(8,128)}) async-done(((f32[512,512]{1,0:T(8,128)}, f32[512,512]{1,0:T(8,128)}), (f32[512,512]{1,0:T(8,128)}, f32[512,512]{1,0:T(8,128)})) %all-reduce.21.cloned.1.call-update) | async-done | bytes 2097168 | tf_op jit(solution)/shard_map/while/body/eval_jaxpr/psum | solution.py:148
  429.6 2.1 fusion.378
  432.8 2.5 fusion.380
  450.5 2.0 convolution_convert_fusion.30
  453.9 32.9 %all-reduce.13.cloned.1.call-done = f32[512,512]{1,0:T(8,128)} async-done(((f32[512,512]{1,0:T(8,128)}), f32[512,512]{1,0:T(8,128)}) %all-reduce.13.cloned.1.call-update) | async-done | bytes 1048592 | tf_op jit(solution)/shard_map/while/body/eval_jaxpr/psum | solution.py:145
  493.6 36.6 %all-reduce.15.cloned.1.call-done = f32[512,512]{1,0:T(8,128)} async-done(((f32[512,512]{1,0:T(8,128)}), f32[512,512]{1,0:T(8,128)}) %all-reduce.15.cloned.1.call-update) | async-done | bytes 1048592 | tf_op jit(solution)/shard_map/while/body/eval_jaxpr/psum | solution.py:145
  532.3 3.6 multiply_convert_fusion.6
  539.2 3.2 convolution_add_fusion.11
  543.9 3.1 convolution_add_fusion.10
  546.9 28.8 %all-reduce.17.cloned.1.call-done = f32[512,512]{1,0:T(8,128)} async-done(((f32[512,512]{1,0:T(8,128)}), f32[512,512]{1,0:T(8,128)}) %all-reduce.17.cloned.1.call-update) | async-done | bytes 1048592 | tf_op jit(solution)/shard_map/while/body/eval_jaxpr/psum | solution.py:148
  575.7 2.5 multiply_reduce_fusion.19
  583.3 2.2 fusion.366
  585.6 2.4 fusion.373
  588.0 2.0 convolution_convert_fusion.35
  590.0 32.2 %all-reduce.19.cloned.1.call-done = f32[512,512]{1,0:T(8,128)} async-done(((f32[512,512]{1,0:T(8,128)}), f32[512,512]{1,0:T(8,128)}) %all-reduce.19.cloned.1.call-update) | async-done | bytes 1048592 | tf_op jit(solution)/shard_map/while/body/eval_jaxpr/psum | solution.py:148
  622.2 2.7 multiply_reduce_fusion.21
  635.5 2.2 convolution_add_fusion.9
  641.7 2.1 fusion.374
  643.8 2.1 fusion.375
  646.1 3.5 select_add_fusion.4
  649.6 43.3 %all-reduce.21.cloned.1.call-done = (f32[512,512]{1,0:T(8,128)}, f32[512,512]{1,0:T(8,128)}) async-done(((f32[512,512]{1,0:T(8,128)}, f32[512,512]{1,0:T(8,128)}), (f32[512,512]{1,0:T(8,128)}, f32[512,512]{1,0:T(8,128)})) %all-reduce.21.cloned.1.call-update) | async-done | bytes 2097168 | tf_op jit(solution)/shard_map/while/body/eval_jaxpr/psum | solution.py:148
  693.0 2.1 fusion.378
  696.1 2.5 fusion.380
  699.4 38.8 %psum.81 = f32[6,512]{1,0:T(8,128)S(1)} all-reduce(f32[6,512]{1,0:T(8,128)S(1)} %copy-done.60), channel_id=1, replica_groups=mesh['dp'=8,'tensor'=4] {'dp'}, use_global_device_ids=true, to_apply=%region_36.37 | all-reduce | flops 3072 | bytes 24576 | tf_op jit(solution)/shard_map/psum | solution.py:242
  738.9 121.8 %all-reduce.11.cloned.1.call-done = (f32[6,512,128]{2,1,0:T(8,128)}, f32[2,512,128]{2,1,0:T(8,128)}, f32[512,512]{1,0:T(8,128)}, f32[512,512]{1,0:T(8,128)}) async-done(((f32[6,512,128]{2,1,0:T(8,128)}, f32[2,512,128]{2,1,0:T(8,128)}, f32[512,512]{1,0:T(8,128)}, f32[512,512]{1,0:T(8,128)}), (f32[6,512,128]{2,1,0:T(8,128)}, f32[2,512,128]{2,1,0:T(8,128)}, f32[512,512]{1,0:T(8,128)}, ...) | async-done | bytes 4194320 | tf_op jit(solution)/shard_map/psum | solution.py:242
  (474 shorter events, 111.1 us)
Async XLA Ops:
  8.0 164.3 %copy-start.8 = (bf16[1024,512]{1,0:T(8,128)(2,1)S(1)}, bf16[1024,512]{1,0:T(8,128)(2,1)}, u32[]{:S(2)}) copy-start(bf16[1024,512]{1,0:T(8,128)(2,1)} %param.22) | copy-start | bytes 3145732
  172.3 51.0 %all-reduce.13.cloned.1.call-start = ((), (), s32[]{:S(2)}) async-start(), calls=%async_computation.1 | async-start | bytes 2097152 | tf_op jit(solution)/shard_map/while/body/eval_jaxpr/psum | solution.py:145
  172.8 12.0 %copy-start.46 = (f32[512]{0:T(512)}, f32[512]{0:T(512)S(1)}, u32[]{:S(2)}) copy-start(f32[512]{0:T(512)S(1)} %add_rsqrt_fusion.6) | copy-start | bytes 6148 | tf_op jit(solution)/shard_map/while
  174.4 10.4 %copy-start.48 = (f32[1,512]{1,0:T(1,128)}, f32[1,512]{1,0:T(1,128)S(1)}, u32[]{:S(2)}) copy-start(f32[1,512]{1,0:T(1,128)S(1)} %get-tuple-element.436) | copy-start | bytes 6148 | tf_op jit(solution)/shard_map/while
  174.4 50.7 %copy-start.50 = (f32[1,512]{1,0:T(1,128)}, f32[1,512]{1,0:T(1,128)S(1)}, u32[]{:S(2)}) copy-start(f32[1,512]{1,0:T(1,128)S(1)} %get-tuple-element.442) | copy-start | bytes 6148 | tf_op jit(solution)/shard_map/while
  176.0 9.1 %copy-start.20 = (bf16[512,128]{0,1:T(8,128)(2,1)}, bf16[512,128]{0,1:T(8,128)(2,1)S(1)}, u32[]{:S(2)}) copy-start(bf16[512,128]{0,1:T(8,128)(2,1)S(1)} %convolution_convert_fusion.26) | copy-start | bytes 393220 | tf_op jit(solution)/shard_map/while
  177.3 7.8 copy-start.42
  186.1 38.6 %copy-start.22 = (bf16[2,64,512]{2,1,0:T(8,128)(2,1)}, bf16[2,64,512]{2,1,0:T(8,128)(2,1)S(1)}, u32[]{:S(2)}) copy-start(bf16[2,64,512]{2,1,0:T(8,128)(2,1)S(1)} %convolution_convert_fusion.27) | copy-start | bytes 393220 | tf_op jit(solution)/shard_map/while
  187.5 79.3 %all-reduce.15.cloned.1.call-start = ((), (), s32[]{:S(2)}) async-start(), calls=%async_computation.2 | async-start | bytes 2097152 | tf_op jit(solution)/shard_map/while/body/eval_jaxpr/psum | solution.py:145
  230.2 82.2 %all-reduce.17.cloned.1.call-start = ((), (), s32[]{:S(2)}) async-start(), calls=%async_computation.3 | async-start | bytes 2097152 | tf_op jit(solution)/shard_map/while/body/eval_jaxpr/psum | solution.py:148
  275.7 83.1 %all-reduce.19.cloned.1.call-start = ((), (), s32[]{:S(2)}) async-start(), calls=%async_computation.4 | async-start | bytes 2097152 | tf_op jit(solution)/shard_map/while/body/eval_jaxpr/psum | solution.py:148
  322.2 107.4 %all-reduce.21.cloned.1.call-start = ((), (), s32[]{:S(2)}) async-start(), calls=%async_computation.5 | async-start | bytes 4194304 | tf_op jit(solution)/shard_map/while/body/eval_jaxpr/psum | solution.py:148
  326.6 34.9 %copy-start.3 = (f32[512,512]{1,0:T(8,128)S(1)}, f32[512,512]{1,0:T(8,128)}, u32[]{:S(2)}) copy-start(f32[512,512]{1,0:T(8,128)} %copy-done.2) | copy-start | bytes 3145732 | tf_op jit(solution)/shard_map/while
  326.6 34.9 %copy-start.51 = (f32[1,512]{1,0:T(1,128)S(1)}, f32[1,512]{1,0:T(1,128)}, u32[]{:S(2)}) copy-start(f32[1,512]{1,0:T(1,128)} %copy-done.50) | copy-start | bytes 6148 | tf_op jit(solution)/shard_map/while
  382.7 46.9 %copy-start.47 = (f32[512]{0:T(512)S(1)}, f32[512]{0:T(512)}, u32[]{:S(2)}) copy-start(f32[512]{0:T(512)} %copy-done.46) | copy-start | bytes 6148 | tf_op jit(solution)/shard_map/while
  382.7 46.9 %copy-start.49 = (f32[1,512]{1,0:T(1,128)S(1)}, f32[1,512]{1,0:T(1,128)}, u32[]{:S(2)}) copy-start(f32[1,512]{1,0:T(1,128)} %copy-done.48) | copy-start | bytes 6148 | tf_op jit(solution)/shard_map/while
  435.3 51.5 %all-reduce.13.cloned.1.call-start = ((), (), s32[]{:S(2)}) async-start(), calls=%async_computation.1 | async-start | bytes 2097152 | tf_op jit(solution)/shard_map/while/body/eval_jaxpr/psum | solution.py:145
  435.7 12.0 %copy-start.46 = (f32[512]{0:T(512)}, f32[512]{0:T(512)S(1)}, u32[]{:S(2)}) copy-start(f32[512]{0:T(512)S(1)} %add_rsqrt_fusion.6) | copy-start | bytes 6148 | tf_op jit(solution)/shard_map/while
  437.3 10.4 %copy-start.48 = (f32[1,512]{1,0:T(1,128)}, f32[1,512]{1,0:T(1,128)S(1)}, u32[]{:S(2)}) copy-start(f32[1,512]{1,0:T(1,128)S(1)} %get-tuple-element.436) | copy-start | bytes 6148 | tf_op jit(solution)/shard_map/while
  437.3 51.2 %copy-start.50 = (f32[1,512]{1,0:T(1,128)}, f32[1,512]{1,0:T(1,128)S(1)}, u32[]{:S(2)}) copy-start(f32[1,512]{1,0:T(1,128)S(1)} %get-tuple-element.442) | copy-start | bytes 6148 | tf_op jit(solution)/shard_map/while
  438.9 9.1 %copy-start.20 = (bf16[512,128]{0,1:T(8,128)(2,1)}, bf16[512,128]{0,1:T(8,128)(2,1)S(1)}, u32[]{:S(2)}) copy-start(bf16[512,128]{0,1:T(8,128)(2,1)S(1)} %convolution_convert_fusion.26) | copy-start | bytes 393220 | tf_op jit(solution)/shard_map/while
  440.2 7.8 copy-start.42
  449.1 39.1 %copy-start.22 = (bf16[2,64,512]{2,1,0:T(8,128)(2,1)}, bf16[2,64,512]{2,1,0:T(8,128)(2,1)S(1)}, u32[]{:S(2)}) copy-start(bf16[2,64,512]{2,1,0:T(8,128)(2,1)S(1)} %convolution_convert_fusion.27) | copy-start | bytes 393220 | tf_op jit(solution)/shard_map/while
  450.4 79.8 %all-reduce.15.cloned.1.call-start = ((), (), s32[]{:S(2)}) async-start(), calls=%async_computation.2 | async-start | bytes 2097152 | tf_op jit(solution)/shard_map/while/body/eval_jaxpr/psum | solution.py:145
  493.5 82.2 %all-reduce.17.cloned.1.call-start = ((), (), s32[]{:S(2)}) async-start(), calls=%async_computation.3 | async-start | bytes 2097152 | tf_op jit(solution)/shard_map/while/body/eval_jaxpr/psum | solution.py:148
  539.1 83.1 %all-reduce.19.cloned.1.call-start = ((), (), s32[]{:S(2)}) async-start(), calls=%async_computation.4 | async-start | bytes 2097152 | tf_op jit(solution)/shard_map/while/body/eval_jaxpr/psum | solution.py:148
  585.5 107.4 %all-reduce.21.cloned.1.call-start = ((), (), s32[]{:S(2)}) async-start(), calls=%async_computation.5 | async-start | bytes 4194304 | tf_op jit(solution)/shard_map/while/body/eval_jaxpr/psum | solution.py:148
  590.0 34.9 %copy-start.3 = (f32[512,512]{1,0:T(8,128)S(1)}, f32[512,512]{1,0:T(8,128)}, u32[]{:S(2)}) copy-start(f32[512,512]{1,0:T(8,128)} %copy-done.2) | copy-start | bytes 3145732 | tf_op jit(solution)/shard_map/while
  590.0 34.9 %copy-start.51 = (f32[1,512]{1,0:T(1,128)S(1)}, f32[1,512]{1,0:T(1,128)}, u32[]{:S(2)}) copy-start(f32[1,512]{1,0:T(1,128)} %copy-done.50) | copy-start | bytes 6148 | tf_op jit(solution)/shard_map/while
  628.7 6.8 copy-start.18
  646.1 46.9 %copy-start.47 = (f32[512]{0:T(512)S(1)}, f32[512]{0:T(512)}, u32[]{:S(2)}) copy-start(f32[512]{0:T(512)} %copy-done.46) | copy-start | bytes 6148 | tf_op jit(solution)/shard_map/while
  646.1 46.9 %copy-start.49 = (f32[1,512]{1,0:T(1,128)S(1)}, f32[1,512]{1,0:T(1,128)}, u32[]{:S(2)}) copy-start(f32[1,512]{1,0:T(1,128)} %copy-done.48) | copy-start | bytes 6148 | tf_op jit(solution)/shard_map/while
  698.6 162.1 %all-reduce.11.cloned.1.call-start = ((), (), s32[]{:S(2)}) async-start(), calls=%async_computation | async-start | bytes 8388608 | tf_op jit(solution)/shard_map/psum | solution.py:242
  698.7 39.6 %copy-start.81 = (f32[6,64]{1,0:T(8,128)S(1)}, f32[6,64]{1,0:T(8,128)}, u32[]{:S(2)}) copy-start(f32[6,64]{1,0:T(8,128)} %param.31) | copy-start | bytes 4612
  698.7 39.5 %copy-start.82 = (f32[6,64]{1,0:T(8,128)S(1)}, f32[6,64]{1,0:T(8,128)}, u32[]{:S(2)}) copy-start(f32[6,64]{1,0:T(8,128)} %param.41) | copy-start | bytes 4612
  698.7 39.5 %copy-start.83 = (f32[6,64]{1,0:T(8,128)S(1)}, f32[6,64]{1,0:T(8,128)}, u32[]{:S(2)}) copy-start(f32[6,64]{1,0:T(8,128)} %param.36) | copy-start | bytes 4612
  698.7 162.0 %copy-start.57 = (f32[6,64,128]{2,1,0:T(8,128)S(1)}, f32[6,64,128]{2,1,0:T(8,128)}, u32[]{:S(2)}) copy-start(f32[6,64,128]{2,1,0:T(8,128)} %param.27) | copy-start | bytes 589828
  698.7 162.0 %copy-start.71 = (f32[6,64,128]{2,1,0:T(8,128)S(1)}, f32[6,64,128]{2,1,0:T(8,128)}, u32[]{:S(2)}) copy-start(f32[6,64,128]{2,1,0:T(8,128)} %param.37) | copy-start | bytes 589828
  698.7 162.0 %copy-start.72 = (f32[6,64,128]{2,1,0:T(8,128)S(1)}, f32[6,64,128]{2,1,0:T(8,128)}, u32[]{:S(2)}) copy-start(f32[6,64,128]{2,1,0:T(8,128)} %param.32) | copy-start | bytes 589828
  698.7 163.8 %copy-start.64 = (f32[2,64,128]{2,1,0:T(8,128)S(1)}, f32[2,64,128]{2,1,0:T(8,128)}, u32[]{:S(2)}) copy-start(f32[2,64,128]{2,1,0:T(8,128)} %param.28) | copy-start | bytes 196612
  698.8 163.8 %copy-start.79 = (f32[2,64,128]{2,1,0:T(8,128)S(1)}, f32[2,64,128]{2,1,0:T(8,128)}, u32[]{:S(2)}) copy-start(f32[2,64,128]{2,1,0:T(8,128)} %param.38) | copy-start | bytes 196612
  698.8 163.8 %copy-start.80 = (f32[2,64,128]{2,1,0:T(8,128)S(1)}, f32[2,64,128]{2,1,0:T(8,128)}, u32[]{:S(2)}) copy-start(f32[2,64,128]{2,1,0:T(8,128)} %param.33) | copy-start | bytes 196612
  699.2 164.9 %copy-start.61 = (f32[64,512]{1,0:T(8,128)S(1)}, f32[64,512]{1,0:T(8,128)}, u32[]{:S(2)}) copy-start(f32[64,512]{1,0:T(8,128)} %param.29) | copy-start | bytes 393220
  699.2 164.9 %copy-start.62 = (f32[64,512]{1,0:T(8,128)S(1)}, f32[64,512]{1,0:T(8,128)}, u32[]{:S(2)}) copy-start(f32[64,512]{1,0:T(8,128)} %param.30) | copy-start | bytes 393220
  699.2 164.9 %copy-start.73 = (f32[64,512]{1,0:T(8,128)S(1)}, f32[64,512]{1,0:T(8,128)}, u32[]{:S(2)}) copy-start(f32[64,512]{1,0:T(8,128)} %param.40) | copy-start | bytes 393220
  699.2 164.9 %copy-start.74 = (f32[64,512]{1,0:T(8,128)S(1)}, f32[64,512]{1,0:T(8,128)}, u32[]{:S(2)}) copy-start(f32[64,512]{1,0:T(8,128)} %param.35) | copy-start | bytes 393220
  699.2 164.9 %copy-start.75 = (f32[64,512]{1,0:T(8,128)S(1)}, f32[64,512]{1,0:T(8,128)}, u32[]{:S(2)}) copy-start(f32[64,512]{1,0:T(8,128)} %param.34) | copy-start | bytes 393220
  699.3 164.9 %copy-start.76 = (f32[64,512]{1,0:T(8,128)S(1)}, f32[64,512]{1,0:T(8,128)}, u32[]{:S(2)}) copy-start(f32[64,512]{1,0:T(8,128)} %param.39) | copy-start | bytes 393220
  (114 other events, 308.3 us)
Sparse Core Ops, SparseCore 0:
  187.6 35.6 all-reduce.12
  230.3 36.4 all-reduce.14
  275.8 36.4 all-reduce.16
  322.3 36.4 all-reduce.18
  377.6 51.9 all-reduce.20
  450.5 36.1 all-reduce.12
  493.7 36.4 all-reduce.14
  539.2 36.4 all-reduce.16
  585.6 36.4 all-reduce.18
  640.9 51.9 all-reduce.20
Sparse Core Ops, SparseCore 1:
  703.1 157.6 all-reduce.10
where the time goes:
time: 875 us; the launch traced here: 874 us
  waiting for transfers between devices  471 us (54%)
  blocking collectives  198 us (23%)
  matrix products  104 us (12%)
  other arithmetic  61.3 us (7%)
  local copies, waits for them, and re-layouts  19.6 us (2%)
  between operations  15.7 us (2%)
    psum x6, waiting for transfers between devices, sum_grad(): return lax.psum(part_grad, 'tensor')  211 us
    psum x4, waiting for transfers between devices, add_branch(): return resid + lax.psum(part_out, 'tensor')  138 us
    psum x1, waiting for transfers between devices, per_device(): lax.psum((grad_in_all, grad_out_all, grad_norm_all, grad_up, grad_down),...  122 us
    psum x1, blocking collectives, per_device(): lax.psum((grad_in_all, grad_out_all, grad_norm_all, grad_up, grad_down),...  38.8 us
    dot_general x20, matrix products, weight_grad(): lax.dot_general(left_op, right_op, (((0,), (0,)), ((), ())), preferred_el...  33.7 us
    all_gather x1, blocking collectives, per_device(): lax.all_gather(attn_in.astype(low_type), 'dp', axis=1, tiled=True)  33.6 us
    all_gather x1, blocking collectives, per_device(): lax.all_gather(ffn_in.astype(low_type), 'dp', axis=0, tiled=True)  33.6 us
    all_gather x1, blocking collectives, per_device(): lax.all_gather(ffn_out.astype(low_type), 'dp', axis=0, tiled=True)  33.4 us
  transfers between devices with their start and end apart: 11, of which 11 were waited for; matrix products, arithmetic and copies ran while one was open for 5% of the time, Pallas kernels for 0%

commit v1 on v0

--- a/solution.py
+++ b/solution.py
@@ -142,7 +142,7 @@
     gelu_fn = partial(jax.nn.gelu, approximate=False)
 
     def add_branch(resid, part_out):
-        return resid + lax.psum(part_out, "tensor")
+        return resid + jnp.sum(lax.all_gather(part_out, "tensor"), axis=0)
 
     def sum_grad(part_grad):
         return lax.psum(part_grad, "tensor")

time: 875 us -> 901 us (1.030)
  waiting for transfers between devices: 471 us -> 505 us
  matrix products: 104 us -> 83.5 us
  other arithmetic: 61.3 us -> 78.2 us
    all_gather x0 -> x6, waiting for transfers between devices: none -> 198 us  [add_branch(): return resid + jnp.sum(lax.all_gather(part_out, 'tensor'), axis=0)]
    psum x4 -> x0, waiting for transfers between devices: 138 us -> none  [add_branch(): return resid + lax.psum(part_out, 'tensor')]
    psum x6, waiting for transfers between devices: 211 us -> 185 us  [sum_grad(): return lax.psum(part_grad, 'tensor')]
    reduce_sum x0 -> x6, other arithmetic: none -> 20.9 us  [add_branch(): return resid + jnp.sum(lax.all_gather(part_out, 'tensor'), axis=0)]
    dot_general x20, matrix products: 33.7 us -> 18.9 us  [weight_grad(): lax.dot_general(left_op, right_op, (((0,), (0,)), ((), ())), preferred_el...]
  transfers between devices with their start and end apart: 11 -> 13, of which waited for: 11 -> 13; matrix products, arithmetic and copies ran while one was open for 5% -> 5% of each run, Pallas kernels for 0% -> 0%
where the time goes in v1:
time: 901 us; the launch traced here: 900 us
  waiting for transfers between devices  505 us (56%)
  blocking collectives  198 us (22%)
  matrix products  83.5 us (9%)
  other arithmetic  78.2 us (9%)
  between operations  15.8 us (2%)
  local copies, waits for them, and re-layouts  14.8 us (2%)
    all_gather x6, waiting for transfers between devices, add_branch(): return resid + jnp.sum(lax.all_gather(part_out, 'tensor'), axis=0)  198 us
    psum x6, waiting for transfers between devices, sum_grad(): return lax.psum(part_grad, 'tensor')  185 us
    psum x1, waiting for transfers between devices, per_device(): lax.psum((grad_in_all, grad_out_all, grad_norm_all, grad_up, grad_down),...  122 us
    psum x1, blocking collectives, per_device(): lax.psum((grad_in_all, grad_out_all, grad_norm_all, grad_up, grad_down),...  38.8 us
    all_gather x1, blocking collectives, per_device(): lax.all_gather(attn_in.astype(low_type), 'dp', axis=1, tiled=True)  33.6 us
    all_gather x1, blocking collectives, per_device(): lax.all_gather(ffn_in.astype(low_type), 'dp', axis=0, tiled=True)  33.6 us
    all_gather x1, blocking collectives, per_device(): lax.all_gather(ffn_out.astype(low_type), 'dp', axis=0, tiled=True)  33.4 us
    all_gather x1, blocking collectives, per_device(): lax.all_gather(attn_out.astype(low_type), 'dp', axis=1, tiled=True)  30.9 us
  transfers between devices with their start and end apart: 13, of which 13 were waited for; matrix products, arithmetic and copies ran while one was open for 5% of the time, Pallas kernels for 0%

profile of v1, /device:TPU:0, one launch (start us, length us, event | category | flops | bytes accessed | tf_op | source)
XLA Modules:
  0.0 899.7 jit_solution(4953580311183122224)
XLA Ops:
  8.9 27.8 %all-gather.3 = bf16[8,64,6]{1,2,0:T(8,128)(2,1)S(1)} all-gather(bf16[1,64,6]{1,2,0:T(8,128)(2,1)S(1)} %convert_bitcast_fusion.1), channel_id=1, replica_groups=mesh['dp'=8,'tensor'=4] {'dp'}, dimensions={0}, use_global_device_ids=true | all-gather | bytes 6912 | tf_op jit(solution)/shard_map/all_gather | solution.py:135
  40.4 30.9 %all_gather.35 = bf16[2,512,128]{2,1,0:T(8,128)(2,1)S(1)} all-gather(bf16[2,64,128]{2,1,0:T(8,128)(2,1)S(1)} %convert_element_type.207), channel_id=1, replica_groups=mesh['dp'=8,'tensor'=4] {'dp'}, dimensions={1}, use_global_device_ids=true | all-gather | bytes 294912 | tf_op jit(solution)/shard_map/all_gather | solution.py:134
  71.2 33.4 %all_gather.37 = bf16[512,512]{1,0:T(8,128)(2,1)} all-gather(bf16[64,512]{1,0:T(8,128)(2,1)S(1)} %convert_element_type.209), channel_id=1, replica_groups=mesh['dp'=8,'tensor'=4] {'dp'}, dimensions={0}, use_global_device_ids=true | all-gather | bytes 589824 | tf_op jit(solution)/shard_map/all_gather | solution.py:139
  104.6 33.6 %all_gather.36 = bf16[512,512]{1,0:T(8,128)(2,1)} all-gather(bf16[64,512]{1,0:T(8,128)(2,1)S(1)} %convert_element_type.208), channel_id=1, replica_groups=mesh['dp'=8,'tensor'=4] {'dp'}, dimensions={0}, use_global_device_ids=true | all-gather | bytes 589824 | tf_op jit(solution)/shard_map/all_gather | solution.py:138
  138.2 33.6 %all_gather.34 = bf16[6,512,128]{2,1,0:T(8,128)(2,1)} all-gather(bf16[6,64,128]{2,1,0:T(8,128)(2,1)S(1)} %convert_element_type.206), channel_id=1, replica_groups=mesh['dp'=8,'tensor'=4] {'dp'}, dimensions={1}, use_global_device_ids=true | all-gather | bytes 884736 | tf_op jit(solution)/shard_map/all_gather | solution.py:133
  171.8 553.0 %while.23 = (s32[]{:T(128)}, f32[6,512,128]{2,1,0:T(8,128)}, f32[2,512,128]{2,1,0:T(8,128)}, f32[6,512]{1,0:T(8,128)}, f32[512,512]{1,0:T(8,128)}, /*index=5*/f3...) while((s32[]{:T(128)}, f32[6,512,128]{2,1,0:T(8,128)}, ...), condition=%wide.region_31.32_spmd.clone, body=%wide.region_0.31_spmd.clone.sunk | while | flops 3966373888 | bytes 339388800 | solution.py:240
  179.0 1.9 fusion.357
  187.3 31.4 %all-gather.17.cloned.1.call-done = f32[2048,512]{1,0:T(8,128)} async-done(((f32[512,512]{1,0:T(8,128)}), f32[2048,512]{1,0:T(8,128)}) %all-gather.17.cloned.1.call-update) | async-done | bytes 4194320 | tf_op jit(solution)/shard_map/while/body/eval_jaxpr/all_gather | solution.py:145
  218.6 2.8 reduce_sum.316
  227.1 34.6 %all-gather.19.cloned.1.call-done = f32[2048,512]{1,0:T(8,128)} async-done(((f32[512,512]{1,0:T(8,128)}), f32[2048,512]{1,0:T(8,128)}) %all-gather.19.cloned.1.call-update) | async-done | bytes 4194320 | tf_op jit(solution)/shard_map/while/body/eval_jaxpr/all_gather | solution.py:145
  261.7 3.7 reduce_sum.317
  267.5 3.6 multiply_convert_fusion.6
  274.3 36.2 %all-reduce.8.cloned.1.call-done = f32[512,512]{1,0:T(8,128)} async-done(((f32[512,512]{1,0:T(8,128)}), f32[512,512]{1,0:T(8,128)}) %all-reduce.8.cloned.1.call-update) | async-done | bytes 1048592 | tf_op jit(solution)/shard_map/while/body/eval_jaxpr/psum | solution.py:148
  310.6 2.5 multiply_reduce_fusion.19
  317.1 2.2 fusion.369
  319.4 36.6 %all-reduce.10.cloned.1.call-done = f32[512,512]{1,0:T(8,128)} async-done(((f32[512,512]{1,0:T(8,128)}), f32[512,512]{1,0:T(8,128)}) %all-reduce.10.cloned.1.call-update) | async-done | bytes 1048592 | tf_op jit(solution)/shard_map/while/body/eval_jaxpr/psum | solution.py:148
  356.0 2.8 multiply_reduce_fusion.21
  366.4 2.2 convolution_add_fusion.9
  368.7 2.7 fusion.381
  371.4 2.9 convolution_add_fusion.11
  384.8 20.4 %all-reduce.12.cloned.1.call-done = f32[512,512]{1,0:T(8,128)} async-done(((f32[512,512]{1,0:T(8,128)}), f32[512,512]{1,0:T(8,128)}) %all-reduce.12.cloned.1.call-update) | async-done | bytes 1048592 | tf_op jit(solution)/shard_map/while/body/eval_jaxpr/psum | solution.py:148
  405.3 1.9 fusion.380
  408.7 33.0 %all-gather.21.cloned.1.call-done = f32[2048,512]{1,0:T(8,128)} async-done(((f32[512,512]{1,0:T(8,128)}), f32[2048,512]{1,0:T(8,128)}) %all-gather.21.cloned.1.call-update) | async-done | bytes 4194320 | tf_op jit(solution)/shard_map/while/body/eval_jaxpr/all_gather | solution.py:145
  441.7 3.9 reduce_sum.318
  445.6 2.5 fusion.382
  455.3 1.9 fusion.357
  463.6 31.8 %all-gather.17.cloned.1.call-done = f32[2048,512]{1,0:T(8,128)} async-done(((f32[512,512]{1,0:T(8,128)}), f32[2048,512]{1,0:T(8,128)}) %all-gather.17.cloned.1.call-update) | async-done | bytes 4194320 | tf_op jit(solution)/shard_map/while/body/eval_jaxpr/all_gather | solution.py:145
  495.4 2.8 reduce_sum.316
  503.8 34.6 %all-gather.19.cloned.1.call-done = f32[2048,512]{1,0:T(8,128)} async-done(((f32[512,512]{1,0:T(8,128)}), f32[2048,512]{1,0:T(8,128)}) %all-gather.19.cloned.1.call-update) | async-done | bytes 4194320 | tf_op jit(solution)/shard_map/while/body/eval_jaxpr/all_gather | solution.py:145
  538.4 3.7 reduce_sum.317
  544.3 3.6 multiply_convert_fusion.6
  551.1 36.2 %all-reduce.8.cloned.1.call-done = f32[512,512]{1,0:T(8,128)} async-done(((f32[512,512]{1,0:T(8,128)}), f32[512,512]{1,0:T(8,128)}) %all-reduce.8.cloned.1.call-update) | async-done | bytes 1048592 | tf_op jit(solution)/shard_map/while/body/eval_jaxpr/psum | solution.py:148
  587.3 2.5 multiply_reduce_fusion.19
  593.8 2.2 fusion.369
  596.1 36.6 %all-reduce.10.cloned.1.call-done = f32[512,512]{1,0:T(8,128)} async-done(((f32[512,512]{1,0:T(8,128)}), f32[512,512]{1,0:T(8,128)}) %all-reduce.10.cloned.1.call-update) | async-done | bytes 1048592 | tf_op jit(solution)/shard_map/while/body/eval_jaxpr/psum | solution.py:148
  632.7 2.8 multiply_reduce_fusion.21
  643.1 2.2 convolution_add_fusion.9
  645.4 2.7 fusion.381
  648.2 3.2 convolution_add_fusion.11
  660.5 2.9 select_add_fusion.4
  663.4 18.6 %all-reduce.12.cloned.1.call-done = f32[512,512]{1,0:T(8,128)} async-done(((f32[512,512]{1,0:T(8,128)}), f32[512,512]{1,0:T(8,128)}) %all-reduce.12.cloned.1.call-update) | async-done | bytes 1048592 | tf_op jit(solution)/shard_map/while/body/eval_jaxpr/psum | solution.py:148
  682.0 1.9 fusion.380
  685.4 33.0 %all-gather.21.cloned.1.call-done = f32[2048,512]{1,0:T(8,128)} async-done(((f32[512,512]{1,0:T(8,128)}), f32[2048,512]{1,0:T(8,128)}) %all-gather.21.cloned.1.call-update) | async-done | bytes 4194320 | tf_op jit(solution)/shard_map/while/body/eval_jaxpr/all_gather | solution.py:145
  718.4 3.9 reduce_sum.318
  722.3 2.5 fusion.382
  725.6 38.8 %psum.60 = f32[6,512]{1,0:T(8,128)S(1)} all-reduce(f32[6,512]{1,0:T(8,128)S(1)} %copy-done.67), channel_id=1, replica_groups=mesh['dp'=8,'tensor'=4] {'dp'}, use_global_device_ids=true, to_apply=%region_36.37 | all-reduce | flops 3072 | bytes 24576 | tf_op jit(solution)/shard_map/psum | solution.py:242
  765.1 121.7 %all-reduce.6.cloned.1.call-done = (f32[6,512,128]{2,1,0:T(8,128)}, f32[2,512,128]{2,1,0:T(8,128)}, f32[512,512]{1,0:T(8,128)}, f32[512,512]{1,0:T(8,128)}) async-done(((f32[6,512,128]{2,1,0:T(8,128)}, f32[2,512,128]{2,1,0:T(8,128)}, f32[512,512]{1,0:T(8,128)}, f32[512,512]{1,0:T(8,128)}), (f32[6,512,128]{2,1,0:T(8,128)}, f32[2,512,128]{2,1,0:T(8,128)}, f32[512,512]{1,0:T(8,128)}, ...) | async-done | bytes 4194320 | tf_op jit(solution)/shard_map/psum | solution.py:242
  890.3 2.0 multiply_add_fusion.3
  (522 shorter events, 101.4 us)
Async XLA Ops:
  8.0 163.7 %copy-start.92 = (s32[2]{0:T(128)S(1)}, s32[2]{0:T(128)}, u32[]{:S(2)}) copy-start(s32[2]{0:T(128)} %param.26) | copy-start | bytes 28
  8.0 163.7 %copy-start.90 = (s32[2]{0:T(128)S(1)}, s32[2]{0:T(128)}, u32[]{:S(2)}) copy-start(s32[2]{0:T(128)} %param.25) | copy-start | bytes 28
  8.0 163.7 %copy-start.6 = (bf16[1024,512]{1,0:T(8,128)(2,1)S(1)}, bf16[1024,512]{1,0:T(8,128)(2,1)}, u32[]{:S(2)}) copy-start(bf16[1024,512]{1,0:T(8,128)(2,1)} %param.22) | copy-start | bytes 3145732
  171.8 46.8 %all-gather.17.cloned.1.call-start = ((), (), s32[]{:S(2)}) async-start(), calls=%async_computation.1 | async-start | bytes 5242880 | tf_op jit(solution)/shard_map/while/body/eval_jaxpr/all_gather | solution.py:145
  172.9 49.0 %copy-start.61 = (f32[1,512]{1,0:T(1,128)}, f32[1,512]{1,0:T(1,128)S(1)}, u32[]{:S(2)}) copy-start(f32[1,512]{1,0:T(1,128)S(1)} %get-tuple-element.438) | copy-start | bytes 6148 | tf_op jit(solution)/shard_map/while
  183.0 35.6 %copy-start.36 = (bf16[2,64,512]{2,1,0:T(8,128)(2,1)}, bf16[2,64,512]{2,1,0:T(8,128)(2,1)S(1)}, u32[]{:S(2)}) copy-start(bf16[2,64,512]{2,1,0:T(8,128)(2,1)S(1)} %convolution_convert_fusion.27) | copy-start | bytes 393220 | tf_op jit(solution)/shard_map/while
  184.4 77.3 %all-gather.19.cloned.1.call-start = ((), (), s32[]{:S(2)}) async-start(), calls=%async_computation.2 | async-start | bytes 5242880 | tf_op jit(solution)/shard_map/while/body/eval_jaxpr/all_gather | solution.py:145
  185.8 38.5 %copy-start.42 = (bf16[512,128]{0,1:T(8,128)(2,1)}, bf16[512,128]{0,1:T(8,128)(2,1)S(1)}, u32[]{:S(2)}) copy-start(bf16[512,128]{0,1:T(8,128)(2,1)S(1)} %convolution_convert_fusion.30) | copy-start | bytes 393220 | tf_op jit(solution)/shard_map/while
  225.7 36.0 %copy-start.38 = (bf16[2,64,512]{2,1,0:T(8,128)(2,1)}, bf16[2,64,512]{2,1,0:T(8,128)(2,1)S(1)}, u32[]{:S(2)}) copy-start(bf16[2,64,512]{2,1,0:T(8,128)(2,1)S(1)} %convolution_convert_fusion.31) | copy-start | bytes 393220 | tf_op jit(solution)/shard_map/while
  227.0 83.5 %all-reduce.8.cloned.1.call-start = ((), (), s32[]{:S(2)}) async-start(), calls=%async_computation.3 | async-start | bytes 2097152 | tf_op jit(solution)/shard_map/while/body/eval_jaxpr/psum | solution.py:148
  274.3 81.7 %all-reduce.10.cloned.1.call-start = ((), (), s32[]{:S(2)}) async-start(), calls=%async_computation.4 | async-start | bytes 2097152 | tf_op jit(solution)/shard_map/while/body/eval_jaxpr/psum | solution.py:148
  319.3 85.9 %all-reduce.12.cloned.1.call-start = ((), (), s32[]{:S(2)}) async-start(), calls=%async_computation.5 | async-start | bytes 2097152 | tf_op jit(solution)/shard_map/while/body/eval_jaxpr/psum | solution.py:148
  368.7 73.0 %all-gather.21.cloned.1.call-start = ((), (), s32[]{:S(2)}) async-start(), calls=%async_computation.6 | async-start | bytes 5242880 | tf_op jit(solution)/shard_map/while/body/eval_jaxpr/all_gather | solution.py:145
  383.4 23.7 %copy-start.74 = (f32[512]{0:T(512)S(1)}, f32[512]{0:T(512)}, u32[]{:S(2)}) copy-start(f32[512]{0:T(512)} %get-tuple-element.463) | copy-start | bytes 6148 | tf_op jit(solution)/shard_map/while
  383.4 23.8 %copy-start.75 = (f32[512]{0:T(512)S(1)}, f32[512]{0:T(512)}, u32[]{:S(2)}) copy-start(f32[512]{0:T(512)} %get-tuple-element.464) | copy-start | bytes 6148 | tf_op jit(solution)/shard_map/while
  383.4 23.8 %copy-start.76 = (f32[512]{0:T(512)S(1)}, f32[512]{0:T(512)}, u32[]{:S(2)}) copy-start(f32[512]{0:T(512)} %get-tuple-element.461) | copy-start | bytes 6148 | tf_op jit(solution)/shard_map/while
  383.4 23.7 %copy-start.77 = (f32[512]{0:T(512)S(1)}, f32[512]{0:T(512)}, u32[]{:S(2)}) copy-start(f32[512]{0:T(512)} %get-tuple-element.462) | copy-start | bytes 6148 | tf_op jit(solution)/shard_map/while
  383.4 23.8 %copy-start.65 = (f32[6,512]{1,0:T(8,128)S(1)}, f32[6,512]{1,0:T(8,128)}, u32[]{:S(2)}) copy-start(f32[6,512]{1,0:T(8,128)} %get-tuple-element.493) | copy-start | bytes 36868 | tf_op jit(solution)/shard_map/while
  407.3 38.3 %copy-start.66 = (f32[6,512]{1,0:T(8,128)}, f32[6,512]{1,0:T(8,128)S(1)}, u32[]{:S(2)}) copy-start(f32[6,512]{1,0:T(8,128)S(1)} %select_add_fusion.5) | copy-start | bytes 36868 | tf_op jit(solution)/shard_map/while
  448.1 47.2 %all-gather.17.cloned.1.call-start = ((), (), s32[]{:S(2)}) async-start(), calls=%async_computation.1 | async-start | bytes 5242880 | tf_op jit(solution)/shard_map/while/body/eval_jaxpr/all_gather | solution.py:145
  449.2 49.4 %copy-start.61 = (f32[1,512]{1,0:T(1,128)}, f32[1,512]{1,0:T(1,128)S(1)}, u32[]{:S(2)}) copy-start(f32[1,512]{1,0:T(1,128)S(1)} %get-tuple-element.438) | copy-start | bytes 6148 | tf_op jit(solution)/shard_map/while
  459.3 36.0 %copy-start.36 = (bf16[2,64,512]{2,1,0:T(8,128)(2,1)}, bf16[2,64,512]{2,1,0:T(8,128)(2,1)S(1)}, u32[]{:S(2)}) copy-start(bf16[2,64,512]{2,1,0:T(8,128)(2,1)S(1)} %convolution_convert_fusion.27) | copy-start | bytes 393220 | tf_op jit(solution)/shard_map/while
  460.7 77.7 %all-gather.19.cloned.1.call-start = ((), (), s32[]{:S(2)}) async-start(), calls=%async_computation.2 | async-start | bytes 5242880 | tf_op jit(solution)/shard_map/while/body/eval_jaxpr/all_gather | solution.py:145
  462.2 38.9 %copy-start.42 = (bf16[512,128]{0,1:T(8,128)(2,1)}, bf16[512,128]{0,1:T(8,128)(2,1)S(1)}, u32[]{:S(2)}) copy-start(bf16[512,128]{0,1:T(8,128)(2,1)S(1)} %convolution_convert_fusion.30) | copy-start | bytes 393220 | tf_op jit(solution)/shard_map/while
  502.4 36.0 %copy-start.38 = (bf16[2,64,512]{2,1,0:T(8,128)(2,1)}, bf16[2,64,512]{2,1,0:T(8,128)(2,1)S(1)}, u32[]{:S(2)}) copy-start(bf16[2,64,512]{2,1,0:T(8,128)(2,1)S(1)} %convolution_convert_fusion.31) | copy-start | bytes 393220 | tf_op jit(solution)/shard_map/while
  503.7 83.5 %all-reduce.8.cloned.1.call-start = ((), (), s32[]{:S(2)}) async-start(), calls=%async_computation.3 | async-start | bytes 2097152 | tf_op jit(solution)/shard_map/while/body/eval_jaxpr/psum | solution.py:148
  551.0 81.7 %all-reduce.10.cloned.1.call-start = ((), (), s32[]{:S(2)}) async-start(), calls=%async_computation.4 | async-start | bytes 2097152 | tf_op jit(solution)/shard_map/while/body/eval_jaxpr/psum | solution.py:148
  596.1 85.9 %all-reduce.12.cloned.1.call-start = ((), (), s32[]{:S(2)}) async-start(), calls=%async_computation.5 | async-start | bytes 2097152 | tf_op jit(solution)/shard_map/while/body/eval_jaxpr/psum | solution.py:148
  645.4 73.0 %all-gather.21.cloned.1.call-start = ((), (), s32[]{:S(2)}) async-start(), calls=%async_computation.6 | async-start | bytes 5242880 | tf_op jit(solution)/shard_map/while/body/eval_jaxpr/all_gather | solution.py:145
  660.5 23.4 %copy-start.75 = (f32[512]{0:T(512)S(1)}, f32[512]{0:T(512)}, u32[]{:S(2)}) copy-start(f32[512]{0:T(512)} %get-tuple-element.464) | copy-start | bytes 6148 | tf_op jit(solution)/shard_map/while
  660.5 23.5 %copy-start.65 = (f32[6,512]{1,0:T(8,128)S(1)}, f32[6,512]{1,0:T(8,128)}, u32[]{:S(2)}) copy-start(f32[6,512]{1,0:T(8,128)} %get-tuple-element.493) | copy-start | bytes 36868 | tf_op jit(solution)/shard_map/while
  684.0 38.3 %copy-start.66 = (f32[6,512]{1,0:T(8,128)}, f32[6,512]{1,0:T(8,128)S(1)}, u32[]{:S(2)}) copy-start(f32[6,512]{1,0:T(8,128)S(1)} %select_add_fusion.5) | copy-start | bytes 36868 | tf_op jit(solution)/shard_map/while
  724.8 162.0 %all-reduce.6.cloned.1.call-start = ((), (), s32[]{:S(2)}) async-start(), calls=%async_computation | async-start | bytes 8388608 | tf_op jit(solution)/shard_map/psum | solution.py:242
  724.9 39.5 %copy-start.87 = (f32[6,64]{1,0:T(8,128)S(1)}, f32[6,64]{1,0:T(8,128)}, u32[]{:S(2)}) copy-start(f32[6,64]{1,0:T(8,128)} %param.31) | copy-start | bytes 4612
  724.9 39.5 %copy-start.88 = (f32[6,64]{1,0:T(8,128)S(1)}, f32[6,64]{1,0:T(8,128)}, u32[]{:S(2)}) copy-start(f32[6,64]{1,0:T(8,128)} %param.41) | copy-start | bytes 4612
  724.9 39.5 %copy-start.89 = (f32[6,64]{1,0:T(8,128)S(1)}, f32[6,64]{1,0:T(8,128)}, u32[]{:S(2)}) copy-start(f32[6,64]{1,0:T(8,128)} %param.36) | copy-start | bytes 4612
  724.9 161.9 %copy-start.64 = (f32[6,64,128]{2,1,0:T(8,128)S(1)}, f32[6,64,128]{2,1,0:T(8,128)}, u32[]{:S(2)}) copy-start(f32[6,64,128]{2,1,0:T(8,128)} %param.27) | copy-start | bytes 589828
  724.9 161.9 %copy-start.79 = (f32[6,64,128]{2,1,0:T(8,128)S(1)}, f32[6,64,128]{2,1,0:T(8,128)}, u32[]{:S(2)}) copy-start(f32[6,64,128]{2,1,0:T(8,128)} %param.37) | copy-start | bytes 589828
  724.9 161.9 %copy-start.80 = (f32[6,64,128]{2,1,0:T(8,128)S(1)}, f32[6,64,128]{2,1,0:T(8,128)}, u32[]{:S(2)}) copy-start(f32[6,64,128]{2,1,0:T(8,128)} %param.32) | copy-start | bytes 589828
  724.9 163.7 %copy-start.73 = (f32[2,64,128]{2,1,0:T(8,128)S(1)}, f32[2,64,128]{2,1,0:T(8,128)}, u32[]{:S(2)}) copy-start(f32[2,64,128]{2,1,0:T(8,128)} %param.28) | copy-start | bytes 196612
  725.0 163.7 %copy-start.85 = (f32[2,64,128]{2,1,0:T(8,128)S(1)}, f32[2,64,128]{2,1,0:T(8,128)}, u32[]{:S(2)}) copy-start(f32[2,64,128]{2,1,0:T(8,128)} %param.38) | copy-start | bytes 196612
  725.0 163.7 %copy-start.86 = (f32[2,64,128]{2,1,0:T(8,128)S(1)}, f32[2,64,128]{2,1,0:T(8,128)}, u32[]{:S(2)}) copy-start(f32[2,64,128]{2,1,0:T(8,128)} %param.33) | copy-start | bytes 196612
  725.4 164.8 %copy-start.68 = (f32[64,512]{1,0:T(8,128)S(1)}, f32[64,512]{1,0:T(8,128)}, u32[]{:S(2)}) copy-start(f32[64,512]{1,0:T(8,128)} %param.29) | copy-start | bytes 393220
  725.4 164.8 %copy-start.69 = (f32[64,512]{1,0:T(8,128)S(1)}, f32[64,512]{1,0:T(8,128)}, u32[]{:S(2)}) copy-start(f32[64,512]{1,0:T(8,128)} %param.30) | copy-start | bytes 393220
  725.4 164.8 %copy-start.81 = (f32[64,512]{1,0:T(8,128)S(1)}, f32[64,512]{1,0:T(8,128)}, u32[]{:S(2)}) copy-start(f32[64,512]{1,0:T(8,128)} %param.40) | copy-start | bytes 393220
  725.4 164.8 %copy-start.82 = (f32[64,512]{1,0:T(8,128)S(1)}, f32[64,512]{1,0:T(8,128)}, u32[]{:S(2)}) copy-start(f32[64,512]{1,0:T(8,128)} %param.35) | copy-start | bytes 393220
  725.4 164.8 %copy-start.83 = (f32[64,512]{1,0:T(8,128)S(1)}, f32[64,512]{1,0:T(8,128)}, u32[]{:S(2)}) copy-start(f32[64,512]{1,0:T(8,128)} %param.34) | copy-start | bytes 393220
  725.5 164.8 %copy-start.84 = (f32[64,512]{1,0:T(8,128)S(1)}, f32[64,512]{1,0:T(8,128)}, u32[]{:S(2)}) copy-start(f32[64,512]{1,0:T(8,128)} %param.39) | copy-start | bytes 393220
  (134 other events, 521.9 us)
Sparse Core Ops, SparseCore 0:
  184.5 34.0 all-gather.16
  227.1 34.4 all-gather.18
  274.4 36.1 all-reduce.7
  319.5 36.4 all-reduce.9
  368.8 36.4 all-reduce.11
  406.8 34.8 all-gather.20
  460.8 34.4 all-gather.16
  503.9 34.4 all-gather.18
  551.1 36.1 all-reduce.7
  596.2 36.4 all-reduce.9
  645.5 36.4 all-reduce.11
  683.5 34.8 all-gather.20
Sparse Core Ops, SparseCore 1:
  729.3 157.5 all-reduce.5
